TPU v7x, 256 devices: a whole 4x4x8 slice. The times are simulated.
256 devices in a mesh: row: 4 (over z_hi), col: 16 (over x, y), layer: 4 (over z_lo, core).
Axes of the slice: x: 4, y: 4, z: 8 (z_hi: 4, z_lo: 2; z = z_hi * 2 + z_lo), core: 2. Of those that a mesh axis runs over, the one named last changes fastest.
Arguments:
- a_tiles: bfloat16 [4, 4, 16, 8, 4096], P('row', 'layer', 'col'), may hold values from -6 to 6
- b_tiles: bfloat16 [4, 4, 16, 16, 4096], P('layer', 'row', 'col'), may hold values from -0.25 to 0.25
- a_slots: int32 [4, 16, 4, 768], P('row', 'col', 'layer'), may hold values from 0 to 128, as said below
- b_slots: int32 [4, 16, 4, 768], P('row', 'col', 'layer'), may hold values from 0 to 63, as said below
Outputs:
- c_tiles: bfloat16 [4, 16, 96, 4096], P('row', 'col', 'layer')
Inputs may be any that keep to these rules, and one draw needn't show every extreme that they name: `a_slots`: entries s * 8 to s * 8 + 7 are the tasks of product tile s; the value 128 marks a dummy task (the zero tile); a tile's live tasks come first, every tile has at least 2 live tasks, and in every list some tile has 8 live tasks and some tile has dummies. `b_slots`: A dummy task holds 0 here.
All inputs are finite; a program needn't handle non-finite values.
Results may differ from a plain program's by a relative error of at most 0.013.
Values may be sent and summed in bfloat16 or wider, within the bound.
A program may use at most 128 MiB of HBM per device.

v0:
```python
import jax
import jax.numpy as jnp
from jax import lax
from jax.sharding import PartitionSpec as P

TILE = 64
TASKS = 8


def tile_sums(a_panel, b_panel, a_index, b_index):
    tiles_here = a_index.shape[0] // TASKS
    a_stack = jnp.take(a_panel, a_index, axis=0).reshape(tiles_here, TASKS, TILE, TILE)
    b_stack = jnp.take(b_panel, b_index, axis=0).reshape(tiles_here, TASKS, TILE, TILE)
    return jnp.einsum("sgik,sgkj->sij", a_stack, b_stack, preferred_element_type=jnp.float32)


def shards(a_tiles, b_tiles, a_slots, b_slots):
    flat = TILE * TILE
    a_local = a_tiles.reshape(-1, flat)
    b_local = b_tiles.reshape(-1, flat)
    a_index = a_slots.reshape(-1)
    b_index = b_slots.reshape(-1)
    layer_count = lax.axis_size("layer")
    zero_tile = jnp.zeros((1, flat), jnp.bfloat16)
    a_panel = lax.all_gather(a_local, "col", axis=0, tiled=True)
    a_panel = jnp.concatenate([a_panel, zero_tile], axis=0)
    b_panel = lax.all_gather(b_local, "row", axis=0, tiled=True)
    owned_tiles = a_index.shape[0] // TASKS // layer_count
    partial_value = tile_sums(a_panel, b_panel, a_index, b_index).reshape(
        owned_tiles * layer_count, flat
    )
    summed = lax.psum_scatter(
        partial_value.astype(jnp.bfloat16), "layer", scatter_dimension=0, tiled=True
    )
    return summed.reshape(1, 1, -1, flat)


def solution(mesh):
    in_specs = (
        P("row", "layer", "col", None, None),
        P("layer", "row", "col", None, None),
        P("row", "col", "layer", None),
        P("row", "col", "layer", None),
    )
    out_specs = P("row", "col", "layer", None)
    return jax.shard_map(shards, mesh=mesh, in_specs=in_specs, out_specs=out_specs, check_vma=False)
```

profile of v0, /device:TPU:1, one launch (start us, length us, event | category | flops | bytes accessed | tf_op | source)
XLA Modules:
  0.0 131.5 jit_solution(2519793150495146761)
XLA Ops:
  6.5 0.0 all-gather.4.cloned.1.call-start
  6.5 0.7 all-gather.4.cloned.1.call-update
  7.3 0.0 reduce-scatter.4.cloned.1.call-start
  7.3 0.7 reduce
  8.0 0.7 reduce.2
  8.7 0.1 reshape.106
  8.8 0.1 reshape.103
  8.9 0.7 fusion.11
  9.6 18.3 %all-gather.1 = bf16[1,1,1,64,4096]{4,3,2,1,0:T(8,128)(2,1)S(1)} all-gather(bf16[1,1,1,16,4096]{4,3,2,1,0:T(8,128)(2,1)} %param.5), channel_id=3, replica_groups=mesh['row'=4,'col'=16,'layer'=4] {'row'}, dimensions={3}, use_global_device_ids=true | all-gather | bytes 655360 | tf_op jit(solution)/shard_map/all_gather | solution.py:27
  27.9 5.7 %gather_fusion.1 = bf16[768,4096]{1,0:T(8,128)(2,1)} fusion(bf16[64,4096]{1,0:T(8,128)(2,1)S(1)} %bitcast.12, s32[1024]{0:T(1024)S(1)} %pad_clamp_fusion), kind=kCustom, calls=%fused_computation.1 | custom fusion | bytes 12585984 | tf_op jit(solution)/shard_map/jit(_take)/gather | solution.py:13
  33.6 0.0 copy-start
  33.6 17.9 %gather.15 = bf16[96,8,64,64]{3,2,1,0:T(8,128)(2,1)} reshape(bf16[768,4096]{1,0:T(8,128)(2,1)} %gather_fusion.1) | data formatting | bytes 12582912 | tf_op jit(solution)/shard_map/jit(_take)/gather | solution.py:13
  51.5 0.0 copy-done
  51.6 8.3 %all-gather.4.cloned.1.call-done = bf16[1,1,1,128,4096]{4,3,2,1,0:T(8,128)(2,1)} async-done(((bf16[1,1,1,8,4096]{4,3,2,1,0:T(8,128)(2,1)}), bf16[1,1,1,128,4096]{4,3,2,1,0:T(8,128)(2,1)}) %all-gather.4.cloned.1.call-update) | async-done | bytes 1048592 | tf_op jit(solution)/shard_map/all_gather | solution.py:25
  59.9 1.3 %concatenate.3 = bf16[129,4096]{1,0:T(8,128)(2,1)S(1)} pad(bf16[128,4096]{1,0:T(8,128)(2,1)} %bitcast.15, bf16[]{:T(256)} %constant.28.clone.1), padding=0_1x0_0 | pad | bytes 2105346 | tf_op jit(solution)/shard_map/concatenate | solution.py:26
  61.2 5.8 %gather_fusion = bf16[768,4096]{1,0:T(8,128)(2,1)} fusion(bf16[129,4096]{1,0:T(8,128)(2,1)S(1)} %concatenate.3, s32[1024]{0:T(1024)S(1)} %pad_clamp_fusion.1), kind=kCustom, calls=%fused_computation | custom fusion | bytes 12585984 | tf_op jit(solution)/shard_map/jit(_take)/gather | solution.py:12
  67.0 17.9 %gather.13 = bf16[96,8,64,64]{3,2,1,0:T(8,128)(2,1)} reshape(bf16[768,4096]{1,0:T(8,128)(2,1)} %gather_fusion) | data formatting | bytes 12582912 | tf_op jit(solution)/shard_map/jit(_take)/gather | solution.py:12
  84.9 11.1 %bitcast_convert_fusion = bf16[96,64,64]{2,1,0:T(8,128)(2,1)S(1)} fusion(bf16[96,8,64,64]{3,2,1,0:T(8,128)(2,1)} %gather.15, pred[96,8]{1,0:T(8,128)(4,1)S(1)} %get-tuple-element.5, bf16[96,8,64,64]{3,2,1,0:T(8,128)(2,1)} %gather.13, pred[96,8]{1,0:T(8,128)(4,1)S(1)} %get-tuple-element.6), kind=kOutput, calls=%fused_computation.8 | convolution fusion | flops 409337856 | bytes 13370880 | tf_op jit(solution)/shard_map/sgik,sgkj->sij/dot_general | solution.py:14
  96.0 1.7 %copy.7 = bf16[96,64,64]{0,2,1:T(8,128)(2,1)S(1)} copy(bf16[96,64,64]{2,1,0:T(8,128)(2,1)S(1)} %bitcast_convert_fusion) | data formatting | bytes 1572864 | tf_op jit(solution)/shard_map/convert_element_type | solution.py:33
  97.8 1.3 copy.10
  99.0 0.0 reduce-scatter.4.cloned.1.call-update
  99.1 23.2 %reduce-scatter.4.cloned.1.call-done = bf16[24,4096]{1,0:T(8,128)(2,1)} async-done(((bf16[96,4096]{1,0:T(8,128)(2,1)}), bf16[24,4096]{1,0:T(8,128)(2,1)}) %reduce-scatter.4.cloned.1.call-update) | async-done | bytes 196624
  122.3 1.4 %copy.11 = bf16[24,4096]{0,1:T(8,128)(2,1)S(1)} copy(bf16[24,4096]{1,0:T(8,128)(2,1)} %reduce-scatter.4.cloned.1.call-done) | data formatting | bytes 393216
  123.7 1.0 copy.8
  (4 shorter events, 0.1 us)
Async XLA Ops:
  6.5 53.4 %all-gather.4.cloned.1.call-start = ((), (), s32[]{:S(2)}) async-start(), calls=%async_computation.1 | async-start | bytes 1114112 | tf_op jit(solution)/shard_map/all_gather | solution.py:25
  7.3 115.0 %reduce-scatter.4.cloned.1.call-start = ((), (), s32[]{:S(2)}) async-start(), calls=%async_computation.2 | async-start | bytes 983040
  33.6 17.9 %copy-start = (s32[1,1,1,768]{3,2,1,0:T(1,128)S(1)}, s32[1,1,1,768]{3,2,1,0:T(1,128)}, u32[]{:S(2)}) copy-start(s32[1,1,1,768]{3,2,1,0:T(1,128)} %param.6) | copy-start | bytes 9220
Sparse Core Ops, SparseCore 0:
  9.8 50.0 all-gather.3
  99.2 23.0 reduce-scatter.3
where the time goes:
time: 133 us; the launch traced here: 132 us
  local copies, waits for them, and re-layouts  54.2 us (41%)
  waiting for transfers between devices  32.3 us (24%)
  blocking collectives  18.3 us (14%)
  between operations  13.5 us (10%)
  matrix products  11.1 us (8%)
  other arithmetic  2.16 us (2%)
    unnamed x3, waiting for transfers between devices  23.9 us
    gather x2, local copies, waits for them, and re-layouts, tile_sums(): jnp.take(a_panel, a_index, axis=0).reshape(tiles_here, TASKS, TILE, TILE)  23.7 us
    gather x2, local copies, waits for them, and re-layouts, tile_sums(): jnp.take(b_panel, b_index, axis=0).reshape(tiles_here, TASKS, TILE, TILE)  23.7 us
    all_gather x1, blocking collectives, shards(): b_panel = lax.all_gather(b_local, 'row', axis=0, tiled=True)  18.3 us
    dot_general x1, matrix products, tile_sums(): jnp.einsum('sgik,sgkj->sij', a_stack, b_stack, preferred_element_type=jnp...  11.1 us
    all_gather x1, waiting for transfers between devices, shards(): a_panel = lax.all_gather(a_local, 'col', axis=0, tiled=True)  8.33 us
    unnamed x4, local copies, waits for them, and re-layouts  2.66 us
  transfers between devices with their start and end apart: 2, of which 2 were waited for; matrix products, arithmetic and copies ran while one was open for 20% of the time, Pallas kernels for 0%

commit v1 on v0

v1 whole, which is shorter than its diff:
```python
import functools

import jax
import jax.numpy as jnp
from jax import lax
from jax.experimental import pallas as pl
from jax.experimental.pallas import tpu as pltpu
from jax.sharding import PartitionSpec as P

MESH = pl.DeviceIdType.MESH
TILE = 64
TASKS = 8
LANES = 128
PACK = TILE * TILE // LANES
TA = 8
TB = 16
HALF_A = 4
B_CHUNK = 4
OWNED = 24
CHUNK = 6
N_CHUNK = OWNED // CHUNK


def low_half(rows):
    return lax.broadcasted_iota(jnp.int32, (rows, LANES), 1) < TILE


def kernel(
    a_hbm, b_hbm, ai_hbm, bi_hbm, out_ref,
    a_raw, b_raw, ai, bi, a_wide, b_wide, b_mix, panel_a, panel_b, a_dup, b_dup,
    own_z, own_out, to_peer, from_peer, to_z, from_z, out_wide,
    in_sem, send_a, recv_a, send_b, recv_b, send_p, recv_p, send_z, recv_z,
):
    row = lax.axis_index("row")
    col = lax.axis_index("col")
    layer = lax.axis_index("layer")
    cx, cy = col // 4, col % 4
    zl, core = layer // 2, layer % 2

    def at_x(d):
        return (cx + d) % 4 * 4 + cy

    def at_y(d):
        return cx * 4 + (cy + d) % 4

    def dev(r=row, c=col, l=layer):
        return (r, c, l)

    peer = dev(l=zl * 2 + (1 - core))
    partner = dev(l=(1 - zl) * 2 + core)
    up, down = (row + 1) % 4, (row + 3) % 4

    copies = [
        pltpu.make_async_copy(b_hbm, b_raw, in_sem.at[0]),
        pltpu.make_async_copy(a_hbm, a_raw, in_sem.at[1]),
        pltpu.make_async_copy(ai_hbm, ai, in_sem.at[2]),
        pltpu.make_async_copy(bi_hbm, bi, in_sem.at[3]),
    ]
    for cp in copies:
        cp.start()

    barrier = pltpu.get_barrier_semaphore()
    others = [dev(c=at_x(d)) for d in (1, 2, 3)] + [dev(c=at_y(d)) for d in (1, 2, 3)]
    others += [dev(r=up), dev(r=down), peer, partner]
    for other in others:
        pl.semaphore_signal(barrier, inc=1, device_id=other, device_id_type=MESH)

    copies[0].wait()
    for j in range(PACK):
        b_wide[pl.ds(j * TB, TB)] = b_raw[:, j * LANES:(j + 1) * LANES].astype(jnp.float32)
    low16 = low_half(16)
    for t in range(TB):
        p0 = b_wide[pl.ds(t, 16, stride=TB)]
        p1 = b_wide[pl.ds(16 * TB + t, 16, stride=TB)]
        b_mix[pl.ds(t * PACK, 16, stride=2)] = jnp.where(low16, p0, pltpu.roll(p1, TILE, 1))
        b_mix[pl.ds(t * PACK + 1, 16, stride=2)] = jnp.where(low16, pltpu.roll(p0, TILE, 1), p1)
    for t in range(TB):
        panel_b[row * TB + t] = b_mix[pl.ds(t * PACK, PACK)].astype(jnp.bfloat16)
    copies[1].wait()
    for j in range(PACK):
        a_wide[pl.ds(j * TA, TA)] = a_raw[:, j * LANES:(j + 1) * LANES].astype(jnp.float32)
    for t in range(TA):
        panel_a[col * TA + t] = a_wide[pl.ds(t, PACK, stride=TA)].astype(jnp.bfloat16)

    pl.semaphore_wait(barrier, len(others))

    started = []

    def send(src, dst, ssem, rsem, device):
        cp = pltpu.make_async_remote_copy(
            src, dst, ssem, rsem, device_id=device, device_id_type=MESH
        )
        cp.start()
        started.append(cp)

    def b_part(h, c):
        return panel_b.at[pl.ds(h * TB + c * B_CHUNK, B_CHUNK)]

    def send_b_part(slot, h, c, device):
        send(b_part(h, c), b_part(h, c), send_b.at[slot], recv_b.at[h, c], device)

    def wait_b(h, c):
        pltpu.make_async_copy(b_part(h, c), b_part(h, c), recv_b.at[h, c]).wait()

    def a_part(half, g):
        return panel_a.at[pl.ds(g * TA + half * HALF_A, HALF_A)]

    def send_a_part(slot, half, g, device):
        send(a_part(half, g), a_part(half, g), send_a.at[slot], recv_a.at[half, g], device)

    def wait_a(half, g):
        pltpu.make_async_copy(a_part(half, g), a_part(half, g), recv_a.at[half, g]).wait()

    for i, c in enumerate((0, 1, 2, 3)):
        send_b_part(2 * i, row, c, dev(r=up))
        send_b_part(2 * i + 1, row, 3 - c, dev(r=down))
    slot = 0
    for d in (1, 3, 2):
        send_a_part(slot, 0, col, dev(c=at_x(d)))
        send_a_part(slot + 1, 1, col, dev(c=at_y(d)))
        slot += 2
    for d in (1, 3, 2):
        send_a_part(slot, 0, col, dev(c=at_y(d)))
        send_a_part(slot + 1, 1, col, dev(c=at_x(d)))
        slot += 2

    low32 = low_half(PACK)

    def spread_b(h, c):
        for i in range(B_CHUNK):
            t = h * TB + c * B_CHUNK + i
            q = panel_b[t]
            turned = pltpu.roll(q, TILE, 1)
            b_dup[t, 0:PACK] = jnp.where(low32, q, turned)
            b_dup[t, PACK:TILE] = jnp.where(low32, turned, q)

    def spread_a(half, g):
        for i in range(HALF_A):
            t = g * TA + half * HALF_A + i
            q = panel_a[t]
            turned = pltpu.roll(q, TILE, 1)
            a_dup[t, 0:PACK] = jnp.where(low32, q, turned)
            a_dup[t, PACK:TILE] = jnp.where(low32, turned, q)

    a_dup[16 * TA] = jnp.zeros((TILE, LANES), jnp.bfloat16)
    for half in range(2):
        spread_a(half, col)
    for c in range(4):
        spread_b(row, c)

    for d in (1, 3, 2):
        wait_a(0, at_x(d))
        for e in (1, 3, 2):
            send_a_part(slot, 0, at_x(d), dev(c=at_y(e)))
            slot += 1
        wait_a(1, at_y(d))
        for e in (1, 3, 2):
            send_a_part(slot, 1, at_y(d), dev(c=at_x(e)))
            slot += 1
        if d == 3:
            wait_b(down, 0)
            send_b_part(8, down, 0, dev(r=up))
            wait_b(up, 3)
            send_b_part(9, up, 3, dev(r=down))
    wait_b(down, 1)
    send_b_part(10, down, 1, dev(r=up))
    wait_b(up, 2)
    send_b_part(11, up, 2, dev(r=down))

    for d in (1, 3, 2):
        spread_a(0, at_x(d))
        spread_a(1, at_y(d))
    for c in (0, 1):
        spread_b(down, c)
        spread_b(up, 3 - c)
    for d in (1, 3, 2):
        for e in (0, 1, 3, 2):
            g = (cx + e) % 4 * 4 + (cy + d) % 4
            wait_a(0, g)
            spread_a(0, g)
            g = (cx + d) % 4 * 4 + (cy + e) % 4
            wait_a(1, g)
            spread_a(1, g)
    for c in (2, 3):
        wait_b(down, c)
        spread_b(down, c)
        wait_b(up, 3 - c)
        spread_b(up, 3 - c)
    far = (row + 2) % 4
    for c in (0, 3, 1, 2):
        wait_b(far, c)
        spread_b(far, c)

    copies[2].wait()
    copies[3].wait()
    low64 = low_half(TILE)

    def product(s):
        left = [
            jnp.where(low64, a_dup[ai[0, s * TASKS + 2 * p]], a_dup[ai[0, s * TASKS + 2 * p + 1]])
            for p in range(TASKS // 2)
        ]
        right = [b_dup[bi[0, s * TASKS + e]] for e in range(TASKS)]
        full = jnp.dot(
            jnp.concatenate(left, axis=1),
            jnp.concatenate(right, axis=0),
            preferred_element_type=jnp.float32,
        )
        return jnp.where(low32, full[:PACK], full[PACK:])

    g1 = ((1 - zl) * 2 + (1 - core)) * OWNED
    g2 = ((1 - zl) * 2 + core) * OWNED
    g3 = (zl * 2 + (1 - core)) * OWNED
    g4 = (zl * 2 + core) * OWNED

    def peer_copy(i):
        return pltpu.make_async_remote_copy(
            to_peer.at[pl.ds(i * CHUNK, CHUNK)], from_peer.at[pl.ds(i * CHUNK, CHUNK)],
            send_p.at[i], recv_p.at[i], device_id=peer, device_id_type=MESH,
        )

    def z_copy(i):
        return pltpu.make_async_remote_copy(
            to_z.at[pl.ds(i * CHUNK, CHUNK)], from_z.at[pl.ds(i * CHUNK, CHUNK)],
            send_z.at[i], recv_z.at[i], device_id=partner, device_id_type=MESH,
        )

    def for_peer(i, base):
        for k in range(CHUNK):
            to_peer[i * CHUNK + k] = product(base + (i % N_CHUNK) * CHUNK + k).astype(jnp.bfloat16)
        peer_copy(i).start()

    def send_on(i):
        peer_copy(i).wait_recv()
        for k in range(CHUNK):
            s = i * CHUNK + k
            to_z[s] = (own_z[s] + from_peer[s].astype(jnp.float32)).astype(jnp.bfloat16)
        z_copy(i).start()

    def first(i, carry):
        for_peer(i, g1)
        for k in range(CHUNK):
            own_z[i * CHUNK + k] = product(g2 + i * CHUNK + k)

        @pl.when(i > 0)
        def _():
            send_on(i - 1)
        return carry

    lax.fori_loop(0, N_CHUNK, first, 0)

    def second(i, carry):
        for_peer(N_CHUNK + i, g3)

        @pl.when(i == 0)
        def _():
            send_on(N_CHUNK - 1)
        for k in range(CHUNK):
            own_out[i * CHUNK + k] = product(g4 + i * CHUNK + k)
        return carry

    lax.fori_loop(0, N_CHUNK, second, 0)

    def third(i, carry):
        peer_copy(N_CHUNK + i).wait_recv()
        z_copy(i).wait_recv()
        for k in range(CHUNK):
            s = i * CHUNK + k
            total = own_out[s] + from_peer[OWNED + s].astype(jnp.float32) + from_z[s].astype(jnp.float32)
            out_wide[pl.ds(s, PACK, stride=OWNED)] = total
        return carry

    lax.fori_loop(0, N_CHUNK, third, 0)
    for j in range(PACK):
        out_ref[:, j * LANES:(j + 1) * LANES] = out_wide[pl.ds(j * OWNED, OWNED)].astype(jnp.bfloat16)

    for cp in started:
        cp.wait_send()
    for i in range(2 * N_CHUNK):
        peer_copy(i).wait_send()
    for i in range(N_CHUNK):
        z_copy(i).wait_send()


def shards(a_tiles, b_tiles, a_slots, b_slots):
    flat = TILE * TILE
    bf16, f32 = jnp.bfloat16, jnp.float32
    out = pl.pallas_call(
        kernel,
        out_shape=jax.ShapeDtypeStruct((OWNED, flat), bf16),
        in_specs=[pl.BlockSpec(memory_space=pl.ANY)] * 4,
        out_specs=pl.BlockSpec(memory_space=pltpu.VMEM),
        scratch_shapes=[
            pltpu.VMEM((TA, flat), bf16),
            pltpu.VMEM((TB, flat), bf16),
            pltpu.SMEM((1, 768), jnp.int32),
            pltpu.SMEM((1, 768), jnp.int32),
            pltpu.VMEM((TA * PACK, LANES), f32),
            pltpu.VMEM((TB * PACK, LANES), f32),
            pltpu.VMEM((TB * PACK, LANES), f32),
            pltpu.VMEM((16 * TA, PACK, LANES), bf16),
            pltpu.VMEM((4 * TB, PACK, LANES), bf16),
            pltpu.VMEM((16 * TA + 1, TILE, LANES), bf16),
            pltpu.VMEM((4 * TB, TILE, LANES), bf16),
            pltpu.VMEM((OWNED, PACK, LANES), f32),
            pltpu.VMEM((OWNED, PACK, LANES), f32),
            pltpu.VMEM((2 * OWNED, PACK, LANES), bf16),
            pltpu.VMEM((2 * OWNED, PACK, LANES), bf16),
            pltpu.VMEM((OWNED, PACK, LANES), bf16),
            pltpu.VMEM((OWNED, PACK, LANES), bf16),
            pltpu.VMEM((PACK * OWNED, LANES), f32),
            pltpu.SemaphoreType.DMA((4,)),
            pltpu.SemaphoreType.DMA((30,)),
            pltpu.SemaphoreType.DMA((2, 16)),
            pltpu.SemaphoreType.DMA((12,)),
            pltpu.SemaphoreType.DMA((4, 4)),
            pltpu.SemaphoreType.DMA((2 * N_CHUNK,)),
            pltpu.SemaphoreType.DMA((2 * N_CHUNK,)),
            pltpu.SemaphoreType.DMA((N_CHUNK,)),
            pltpu.SemaphoreType.DMA((N_CHUNK,)),
        ],
        compiler_params=pltpu.CompilerParams(
            collective_id=0, has_side_effects=True, vmem_limit_bytes=60 * 2**20
        ),
        name="purify",
    )(
        a_tiles.reshape(TA, flat), b_tiles.reshape(TB, flat),
        a_slots.reshape(1, -1), b_slots.reshape(1, -1),
    )
    return out.reshape(1, 1, OWNED, flat)


def solution(mesh):
    in_specs = (
        P("row", "layer", "col", None, None),
        P("layer", "row", "col", None, None),
        P("row", "col", "layer", None),
        P("row", "col", "layer", None),
    )
    out_specs = P("row", "col", "layer", None)
    return jax.shard_map(shards, mesh=mesh, in_specs=in_specs, out_specs=out_specs, check_vma=False)
```

time: 133 us -> 31.1 us (0.23); the launches traced: 132 us -> 31 us
  local copies, waits for them, and re-layouts: 54.2 us -> 1.62 us
  waiting for transfers between devices: 32.3 us -> 0 us
  Pallas kernels: 0 us -> 29.4 us
  blocking collectives: 18.3 us -> 0 us
  between operations: 13.5 us -> 0.01 us
  matrix products: 11.1 us -> 0 us
  other arithmetic: 2.16 us -> 0 us
    gather x4 -> x0, local copies, waits for them, and re-layouts: 47.3 us -> none  [the longest x2 23.7 us: tile_sums(): jnp.take(a_panel, a_index, axis=0).reshape(tiles_here, TASKS, TILE, TILE)]
    pallas_call x0 -> x1, Pallas kernels: none -> 29.4 us  [shards(): pl.pallas_call(kernel, out_shape=jax.ShapeDtypeStruct((OWNED, flat), bf16...]
    unnamed x3 -> x0, waiting for transfers between devices: 23.9 us -> none
    all_gather x1 -> x0, blocking collectives: 18.3 us -> none  [shards(): b_panel = lax.all_gather(b_local, 'row', axis=0, tiled=True)]
    dot_general x1 -> x0, matrix products: 11.1 us -> none  [tile_sums(): jnp.einsum('sgik,sgkj->sij', a_stack, b_stack, preferred_element_type=jnp...]
    all_gather x1 -> x0, waiting for transfers between devices: 8.33 us -> none  [shards(): a_panel = lax.all_gather(a_local, 'col', axis=0, tiled=True)]
    convert_element_type x1 -> x0, local copies, waits for them, and re-layouts: 1.73 us -> none  [shards(): partial_value.astype(jnp.bfloat16)]
    unnamed x2 -> x0, other arithmetic: 1.4 us -> none
  transfers between devices with their start and end apart: 2 -> 0, of which waited for: 2 -> 0; matrix products, arithmetic and copies ran while one was open for 20% -> 0% of each run, Pallas kernels for 0% -> 0%
where the time goes in v1:
time: 31.1 us; the launch traced here: 31 us
  Pallas kernels  29.4 us (95%)
  local copies, waits for them, and re-layouts  1.62 us (5%)
    pallas_call x1, Pallas kernels, shards(): pl.pallas_call(kernel, out_shape=jax.ShapeDtypeStruct((OWNED, flat), bf16...  29.4 us
    unnamed x1, local copies, waits for them, and re-layouts  1.62 us

profile of v1, /device:TPU:1, one launch (start us, length us, event | category | flops | bytes accessed | tf_op | source)
XLA Modules:
  0.0 31.0 jit_solution(10990824033618472949)
XLA Ops:
  0.0 29.4 %purify.1 = bf16[24,4096]{1,0:T(8,128)(2,1)} custom-call(bf16[8,4096]{1,0:T(8,128)(2,1)} %bitcast.7, bf16[16,4096]{1,0:T(8,128)(2,1)} %bitcast.6, s32[1,768]{1,0:T(1,128)} %bitcast.8, s32[1,768]{1,0:T(1,128)} %bitcast.9), custom_call_target="tpu_custom_call" | custom-call | tf_op jit(solution)/shard_map/purify/pallas_call | solution.py:288
  29.4 1.6 %copy.6 = bf16[1,1,24,4096]{3,2,1,0:T(8,128)(2,1)} copy(bf16[1,1,24,4096]{3,2,1,0:T(8,128)(2,1)} %bitcast.5) | data formatting | bytes 393216

commit v2 on v1

v2 whole, which is shorter than its diff:
```python
import jax
import jax.numpy as jnp
from jax import lax
from jax.experimental import pallas as pl
from jax.experimental.pallas import tpu as pltpu
from jax.sharding import PartitionSpec as P

MESH = pl.DeviceIdType.MESH
TILE = 64
TASKS = 8
LANES = 128
PACK = TILE * TILE // LANES
TA = 8
TB = 16
A_COLS = 2048
B_COLS = 1024
OWNED = 24
Z_CUTS = ((0, 4), (4, 6), (10, 8), (18, 6))
PEER_CUTS = Z_CUTS + ((24, 12), (36, 12))


def low_half(rows):
    return lax.broadcasted_iota(jnp.int32, (rows, LANES), 1) < TILE


def kernel(
    a_hbm, b_hbm, ai_hbm, bi_hbm, out_ref,
    a_raw, b_raw, ai, bi, a_wide, b_wide, b_mix, panel_a, panel_b, a_dup, b_dup,
    own_z, own_out, to_peer, from_peer, to_z, from_z, out_wide,
    in_sem, send_a, recv_a, send_b, recv_b, send_p, recv_p, send_z, recv_z,
):
    row = lax.axis_index("row")
    col = lax.axis_index("col")
    layer = lax.axis_index("layer")
    cx, cy = col // 4, col % 4
    zl, core = layer // 2, layer % 2

    def at_x(d):
        return (cx + d) % 4 * 4 + cy

    def at_y(d):
        return cx * 4 + (cy + d) % 4

    def dev(r=row, c=col, l=layer):
        return (r, c, l)

    peer = dev(l=zl * 2 + (1 - core))
    partner = dev(l=(1 - zl) * 2 + core)
    up, down = (row + 1) % 4, (row + 3) % 4
    far = (row + 2) % 4

    barrier = pltpu.get_barrier_semaphore()
    others = [dev(c=at_x(d)) for d in (1, 2, 3)] + [dev(c=at_y(d)) for d in (1, 2, 3)]
    others += [dev(r=up), dev(r=down), peer, partner]
    for other in others:
        pl.semaphore_signal(barrier, inc=1, device_id=other, device_id_type=MESH)

    def b_in(c):
        cut = pl.ds(c * B_COLS, B_COLS)
        return pltpu.make_async_copy(b_hbm.at[:, cut], b_raw.at[:, cut], in_sem.at[c])

    def a_in(half):
        cut = pl.ds(half * A_COLS, A_COLS)
        return pltpu.make_async_copy(a_hbm.at[:, cut], a_raw.at[:, cut], in_sem.at[4 + half])

    ai_in = pltpu.make_async_copy(ai_hbm, ai, in_sem.at[6])
    bi_in = pltpu.make_async_copy(bi_hbm, bi, in_sem.at[7])
    for cp in (b_in(0), b_in(3), a_in(0), a_in(1), b_in(1), b_in(2), ai_in, bi_in):
        cp.start()

    low8, low16, low32, low64 = (low_half(n) for n in (8, 16, 32, 64))

    def pack_b(c):
        b_in(c).wait()
        for j in range(8 * c, 8 * c + 8):
            b_wide[pl.ds(j * TB, TB)] = b_raw[:, j * LANES:(j + 1) * LANES].astype(jnp.float32)
        for u in range(8):
            p = b_wide[pl.ds(8 * c * TB + u, 8, stride=TB)]
            q = b_wide[pl.ds(8 * c * TB + u + 8, 8, stride=TB)]
            base = (c * 8 + u) * 16
            b_mix[pl.ds(base, 8, stride=2)] = jnp.where(low8, p, pltpu.roll(q, TILE, 1))
            b_mix[pl.ds(base + 1, 8, stride=2)] = jnp.where(low8, pltpu.roll(p, TILE, 1), q)
        for u in range(8):
            panel_b[row, c, u] = b_mix[pl.ds((c * 8 + u) * 16, 16)].astype(jnp.bfloat16)

    def pack_a(half):
        a_in(half).wait()
        for j in range(16 * half, 16 * half + 16):
            a_wide[pl.ds(j * TA, TA)] = a_raw[:, j * LANES:(j + 1) * LANES].astype(jnp.float32)
        for t in range(TA):
            panel_a[half, col, t] = a_wide[pl.ds(half * 16 * TA + t, 16, stride=TA)].astype(jnp.bfloat16)

    started = []

    def send(src, dst, ssem, rsem, device):
        cp = pltpu.make_async_remote_copy(
            src, dst, ssem, rsem, device_id=device, device_id_type=MESH
        )
        cp.start()
        started.append(cp)

    b_sent, a_sent = [], []

    def send_b_part(h, c, device):
        part = panel_b.at[h, c]
        send(part, part, send_b.at[len(b_sent)], recv_b.at[h, c], device)
        b_sent.append(c)

    def wait_b(h, c):
        part = panel_b.at[h, c]
        pltpu.make_async_copy(part, part, recv_b.at[h, c]).wait()

    def send_a_part(half, g, device):
        part = panel_a.at[half, g]
        send(part, part, send_a.at[len(a_sent)], recv_a.at[half, g], device)
        a_sent.append(half)

    def wait_a(half, g):
        part = panel_a.at[half, g]
        pltpu.make_async_copy(part, part, recv_a.at[half, g]).wait()

    def along_x(half, g):
        for d in (1, 3, 2):
            send_a_part(half, g, dev(c=at_x(d)))

    def along_y(half, g):
        for d in (1, 3, 2):
            send_a_part(half, g, dev(c=at_y(d)))

    def spread_b(h, c):
        rows = pl.ds(16 * c, 16)
        for u in range(8):
            q = panel_b[h, c, u]
            turned = pltpu.roll(q, TILE, 1)
            b_dup[h * TB + u, rows] = jnp.where(low16, q, turned)
            b_dup[h * TB + 8 + u, rows] = jnp.where(low16, turned, q)

    def spread_a(half, g):
        for t in range(TA):
            q = panel_a[half, g, t]
            turned = pltpu.roll(q, TILE, 1)
            a_dup[g * TA + t, pl.ds(16 * half, 16)] = jnp.where(low16, q, turned)
            a_dup[g * TA + t, pl.ds(32 + 16 * half, 16)] = jnp.where(low16, turned, q)

    pack_b(0)
    pack_b(3)
    pl.semaphore_wait(barrier, len(others))
    send_b_part(row, 0, dev(r=up))
    send_b_part(row, 3, dev(r=down))
    pack_a(0)
    along_x(0, col)
    pack_a(1)
    along_y(1, col)
    pack_b(1)
    send_b_part(row, 1, dev(r=up))
    pack_b(2)
    send_b_part(row, 2, dev(r=down))
    along_y(0, col)
    along_x(1, col)
    for c in (2, 3):
        send_b_part(row, c, dev(r=up))
        send_b_part(row, 3 - c, dev(r=down))

    a_dup[16 * TA] = jnp.zeros((TILE, LANES), jnp.bfloat16)
    for half in range(2):
        spread_a(half, col)
    for c in range(4):
        spread_b(row, c)

    def pass_on_a(d):
        wait_a(0, at_x(d))
        along_y(0, at_x(d))
        wait_a(1, at_y(d))
        along_x(1, at_y(d))

    def pass_on_b(c):
        wait_b(down, c)
        send_b_part(down, c, dev(r=up))
        wait_b(up, 3 - c)
        send_b_part(up, 3 - c, dev(r=down))

    pass_on_a(1)
    pass_on_a(3)
    pass_on_b(0)
    pass_on_a(2)
    pass_on_b(1)

    for d in (1, 3, 2):
        spread_a(0, at_x(d))
        spread_a(1, at_y(d))
    for c in (0, 1):
        spread_b(down, c)
        spread_b(up, 3 - c)
    for d in (1, 3, 2):
        for e in (0, 1, 3, 2):
            g = (cx + e) % 4 * 4 + (cy + d) % 4
            wait_a(0, g)
            spread_a(0, g)
            g = (cx + d) % 4 * 4 + (cy + e) % 4
            wait_a(1, g)
            spread_a(1, g)
    for c in (2, 3):
        wait_b(down, c)
        spread_b(down, c)
        wait_b(up, 3 - c)
        spread_b(up, 3 - c)
    for c in (0, 3, 1, 2):
        wait_b(far, c)
        spread_b(far, c)
    ai_in.wait()
    bi_in.wait()

    def product(s):
        left = [
            jnp.where(low64, a_dup[ai[0, s * TASKS + 2 * p]], a_dup[ai[0, s * TASKS + 2 * p + 1]])
            for p in range(TASKS // 2)
        ]
        right = [b_dup[bi[0, s * TASKS + e]] for e in range(TASKS)]
        full = jnp.dot(
            jnp.concatenate(left, axis=1),
            jnp.concatenate(right, axis=0),
            preferred_element_type=jnp.float32,
        )
        return jnp.where(low32, full[:PACK], full[PACK:])

    g1 = ((1 - zl) * 2 + (1 - core)) * OWNED
    g2 = ((1 - zl) * 2 + core) * OWNED
    g3 = (zl * 2 + (1 - core)) * OWNED
    g4 = (zl * 2 + core) * OWNED

    def peer_copy(i):
        first, count = PEER_CUTS[i]
        cut = pl.ds(first, count)
        return pltpu.make_async_remote_copy(
            to_peer.at[cut], from_peer.at[cut], send_p.at[i], recv_p.at[i],
            device_id=peer, device_id_type=MESH,
        )

    def z_copy(i):
        first, count = Z_CUTS[i]
        cut = pl.ds(first, count)
        return pltpu.make_async_remote_copy(
            to_z.at[cut], from_z.at[cut], send_z.at[i], recv_z.at[i],
            device_id=partner, device_id_type=MESH,
        )

    def for_peer(i, base):
        first, count = PEER_CUTS[i]
        for s in range(first, first + count):
            to_peer[s] = product(base + s % OWNED).astype(jnp.bfloat16)
        peer_copy(i).start()

    def for_z(i):
        first, count = Z_CUTS[i]
        for s in range(first, first + count):
            own_z[s] = product(g2 + s)

    def send_on(i):
        first, count = Z_CUTS[i]
        peer_copy(i).wait_recv()
        for s in range(first, first + count):
            to_z[s] = (own_z[s] + from_peer[s].astype(jnp.float32)).astype(jnp.bfloat16)
        z_copy(i).start()

    n_z, n_peer = len(Z_CUTS), len(PEER_CUTS)
    for_peer(0, g1)
    for_z(0)
    for_peer(1, g1)
    for_z(1)
    for_peer(2, g1)
    for_z(2)
    send_on(0)
    send_on(1)
    for_peer(3, g1)
    for_z(3)
    send_on(2)
    send_on(3)
    for i in range(n_z, n_peer):
        for_peer(i, g3)
    for s in range(OWNED):
        own_out[s] = product(g4 + s)
    for i in range(n_z, n_peer):
        peer_copy(i).wait_recv()
        first, count = PEER_CUTS[i]
        for s in range(first, first + count):
            own_out[s - OWNED] += from_peer[s].astype(jnp.float32)
    for i in range(n_z):
        first, count = Z_CUTS[i]
        z_copy(i).wait_recv()
        for s in range(first, first + count):
            out_wide[pl.ds(s, PACK, stride=OWNED)] = own_out[s] + from_z[s].astype(jnp.float32)
    for j in range(PACK):
        out_ref[:, j * LANES:(j + 1) * LANES] = out_wide[pl.ds(j * OWNED, OWNED)].astype(jnp.bfloat16)

    for cp in started:
        cp.wait_send()
    for i in range(n_peer):
        peer_copy(i).wait_send()
    for i in range(n_z):
        z_copy(i).wait_send()


def shards(a_tiles, b_tiles, a_slots, b_slots):
    flat = TILE * TILE
    bf16, f32 = jnp.bfloat16, jnp.float32
    out = pl.pallas_call(
        kernel,
        out_shape=pltpu.VMEM((OWNED, flat), bf16),
        in_specs=[pl.BlockSpec(memory_space=pl.ANY)] * 4,
        out_specs=pl.BlockSpec(memory_space=pltpu.VMEM),
        scratch_shapes=[
            pltpu.VMEM((TA, flat), bf16),
            pltpu.VMEM((TB, flat), bf16),
            pltpu.SMEM((1, 768), jnp.int32),
            pltpu.SMEM((1, 768), jnp.int32),
            pltpu.VMEM((TA * PACK, LANES), f32),
            pltpu.VMEM((TB * PACK, LANES), f32),
            pltpu.VMEM((TB * PACK, LANES), f32),
            pltpu.VMEM((2, 16, TA, 16, LANES), bf16),
            pltpu.VMEM((4, 4, TB // 2, 16, LANES), bf16),
            pltpu.VMEM((16 * TA + 1, TILE, LANES), bf16),
            pltpu.VMEM((4 * TB, TILE, LANES), bf16),
            pltpu.VMEM((OWNED, PACK, LANES), f32),
            pltpu.VMEM((OWNED, PACK, LANES), f32),
            pltpu.VMEM((2 * OWNED, PACK, LANES), bf16),
            pltpu.VMEM((2 * OWNED, PACK, LANES), bf16),
            pltpu.VMEM((OWNED, PACK, LANES), bf16),
            pltpu.VMEM((OWNED, PACK, LANES), bf16),
            pltpu.VMEM((PACK * OWNED, LANES), f32),
            pltpu.SemaphoreType.DMA((8,)),
            pltpu.SemaphoreType.DMA((30,)),
            pltpu.SemaphoreType.DMA((2, 16)),
            pltpu.SemaphoreType.DMA((12,)),
            pltpu.SemaphoreType.DMA((4, 4)),
            pltpu.SemaphoreType.DMA((len(PEER_CUTS),)),
            pltpu.SemaphoreType.DMA((len(PEER_CUTS),)),
            pltpu.SemaphoreType.DMA((len(Z_CUTS),)),
            pltpu.SemaphoreType.DMA((len(Z_CUTS),)),
        ],
        compiler_params=pltpu.CompilerParams(
            collective_id=0, has_side_effects=True, vmem_limit_bytes=60 * 2**20
        ),
        name="purify",
    )(
        a_tiles.reshape(TA, flat), b_tiles.reshape(TB, flat),
        a_slots.reshape(1, -1), b_slots.reshape(1, -1),
    )
    return out.reshape(1, 1, OWNED, flat)


def solution(mesh):
    in_specs = (
        P("row", "layer", "col", None, None),
        P("layer", "row", "col", None, None),
        P("row", "col", "layer", None),
        P("row", "col", "layer", None),
    )
    out_specs = P("row", "col", "layer", None)
    return jax.shard_map(shards, mesh=mesh, in_specs=in_specs, out_specs=out_specs, check_vma=False)
```

time: 31.1 us -> 28.9 us (0.929)
  Pallas kernels: 29.4 us -> 28.1 us
  local copies, waits for them, and re-layouts: 1.62 us -> 0.68 us
    pallas_call x1, Pallas kernels: 29.4 us -> 28.1 us  [shards(): pl.pallas_call(kernel, out_shape=pltpu.VMEM((OWNED, flat), bf16), in_spec...]
    unnamed x1, local copies, waits for them, and re-layouts: 1.62 us -> 0.68 us
where the time goes in v2:
time: 28.9 us; the launch traced here: 28.8 us
  Pallas kernels  28.1 us (97%)
  local copies, waits for them, and re-layouts  0.68 us (2%)
    pallas_call x1, Pallas kernels, shards(): pl.pallas_call(kernel, out_shape=pltpu.VMEM((OWNED, flat), bf16), in_spec...  28.1 us
    unnamed x1, local copies, waits for them, and re-layouts  0.68 us

profile of v2, /device:TPU:1, one launch (start us, length us, event | category | flops | bytes accessed | tf_op | source)
XLA Modules:
  0.0 28.8 jit_solution(14584715406144781736)
XLA Ops:
  0.0 28.1 %purify.1 = bf16[24,4096]{1,0:T(8,128)(2,1)S(1)} custom-call(bf16[8,4096]{1,0:T(8,128)(2,1)} %bitcast.7, bf16[16,4096]{1,0:T(8,128)(2,1)} %bitcast.6, s32[1,768]{1,0:T(1,128)} %bitcast.8, s32[1,768]{1,0:T(1,128)} %bitcast.9), custom_call_target="tpu_custom_call" | custom-call | tf_op jit(solution)/shard_map/purify/pallas_call | solution.py:306
  28.1 0.7 %copy.6 = bf16[1,1,24,4096]{3,2,1,0:T(8,128)(2,1)} copy(bf16[1,1,24,4096]{3,2,1,0:T(8,128)(2,1)S(1)} %bitcast.5) | data formatting | bytes 393216

commit v3 on v2

--- a/solution.py
+++ b/solution.py
@@ -15,6 +15,11 @@
 A_COLS = 2048
 B_COLS = 1024
 OWNED = 24
+N_SEND_A = 30
+HIGH_BY_CROSS = (0, 1, 2)
+LOW_BY_CROSS = (0, 1, 2)
+N_LOW_B = 12 + len(HIGH_BY_CROSS) - len(LOW_BY_CROSS)
+N_HIGH_B = 12 + len(LOW_BY_CROSS) - len(HIGH_BY_CROSS)
 Z_CUTS = ((0, 4), (4, 6), (10, 8), (18, 6))
 PEER_CUTS = Z_CUTS + ((24, 12), (36, 12))
 
@@ -27,7 +32,7 @@
     a_hbm, b_hbm, ai_hbm, bi_hbm, out_ref,
     a_raw, b_raw, ai, bi, a_wide, b_wide, b_mix, panel_a, panel_b, a_dup, b_dup,
     own_z, own_out, to_peer, from_peer, to_z, from_z, out_wide,
-    in_sem, send_a, recv_a, send_b, recv_b, send_p, recv_p, send_z, recv_z,
+    in_sem, ready, send_a, recv_a, send_b, recv_b, send_p, recv_p, send_z, recv_z,
 ):
     row = lax.axis_index("row")
     col = lax.axis_index("col")
@@ -46,13 +51,17 @@
 
     peer = dev(l=zl * 2 + (1 - core))
     partner = dev(l=(1 - zl) * 2 + core)
-    up, down = (row + 1) % 4, (row + 3) % 4
-    far = (row + 2) % 4
+    mate, cross, far = row + 1 - 2 * (row % 2), 3 - row, (row + 2) % 4
+    is_low = row < 2
 
     barrier = pltpu.get_barrier_semaphore()
-    others = [dev(c=at_x(d)) for d in (1, 2, 3)] + [dev(c=at_y(d)) for d in (1, 2, 3)]
-    others += [dev(r=up), dev(r=down), peer, partner]
-    for other in others:
+
+    @pl.when(is_low)
+    def _():
+        pl.semaphore_signal(barrier, inc=1, device_id=dev(r=cross), device_id_type=MESH)
+
+    friends = [dev(r=mate)] + [dev(c=at(d)) for d in (2, 1, 3) for at in (at_x, at_y)] + [partner, peer]
+    for other in friends:
         pl.semaphore_signal(barrier, inc=1, device_id=other, device_id_type=MESH)
 
     def b_in(c):
@@ -90,42 +99,13 @@
         for t in range(TA):
             panel_a[half, col, t] = a_wide[pl.ds(half * 16 * TA + t, 16, stride=TA)].astype(jnp.bfloat16)
 
-    started = []
-
-    def send(src, dst, ssem, rsem, device):
-        cp = pltpu.make_async_remote_copy(
-            src, dst, ssem, rsem, device_id=device, device_id_type=MESH
-        )
-        cp.start()
-        started.append(cp)
-
-    b_sent, a_sent = [], []
-
-    def send_b_part(h, c, device):
-        part = panel_b.at[h, c]
-        send(part, part, send_b.at[len(b_sent)], recv_b.at[h, c], device)
-        b_sent.append(c)
-
     def wait_b(h, c):
         part = panel_b.at[h, c]
         pltpu.make_async_copy(part, part, recv_b.at[h, c]).wait()
 
-    def send_a_part(half, g, device):
-        part = panel_a.at[half, g]
-        send(part, part, send_a.at[len(a_sent)], recv_a.at[half, g], device)
-        a_sent.append(half)
-
     def wait_a(half, g):
         part = panel_a.at[half, g]
         pltpu.make_async_copy(part, part, recv_a.at[half, g]).wait()
-
-    def along_x(half, g):
-        for d in (1, 3, 2):
-            send_a_part(half, g, dev(c=at_x(d)))
-
-    def along_y(half, g):
-        for d in (1, 3, 2):
-            send_a_part(half, g, dev(c=at_y(d)))
 
     def spread_b(h, c):
         rows = pl.ds(16 * c, 16)
@@ -142,71 +122,143 @@
             a_dup[g * TA + t, pl.ds(16 * half, 16)] = jnp.where(low16, q, turned)
             a_dup[g * TA + t, pl.ds(32 + 16 * half, 16)] = jnp.where(low16, turned, q)
 
-    pack_b(0)
-    pack_b(3)
-    pl.semaphore_wait(barrier, len(others))
-    send_b_part(row, 0, dev(r=up))
-    send_b_part(row, 3, dev(r=down))
-    pack_a(0)
-    along_x(0, col)
-    pack_a(1)
-    along_y(1, col)
-    pack_b(1)
-    send_b_part(row, 1, dev(r=up))
-    pack_b(2)
-    send_b_part(row, 2, dev(r=down))
-    along_y(0, col)
-    along_x(1, col)
-    for c in (2, 3):
-        send_b_part(row, c, dev(r=up))
-        send_b_part(row, 3 - c, dev(r=down))
-
-    a_dup[16 * TA] = jnp.zeros((TILE, LANES), jnp.bfloat16)
-    for half in range(2):
-        spread_a(half, col)
-    for c in range(4):
-        spread_b(row, c)
-
-    def pass_on_a(d):
-        wait_a(0, at_x(d))
-        along_y(0, at_x(d))
-        wait_a(1, at_y(d))
-        along_x(1, at_y(d))
-
-    def pass_on_b(c):
-        wait_b(down, c)
-        send_b_part(down, c, dev(r=up))
-        wait_b(up, 3 - c)
-        send_b_part(up, 3 - c, dev(r=down))
-
-    pass_on_a(1)
-    pass_on_a(3)
-    pass_on_b(0)
-    pass_on_a(2)
-    pass_on_b(1)
-
-    for d in (1, 3, 2):
-        spread_a(0, at_x(d))
-        spread_a(1, at_y(d))
-    for c in (0, 1):
-        spread_b(down, c)
-        spread_b(up, 3 - c)
-    for d in (1, 3, 2):
-        for e in (0, 1, 3, 2):
-            g = (cx + e) % 4 * 4 + (cy + d) % 4
-            wait_a(0, g)
-            spread_a(0, g)
-            g = (cx + d) % 4 * 4 + (cy + e) % 4
-            wait_a(1, g)
-            spread_a(1, g)
-    for c in (2, 3):
-        wait_b(down, c)
-        spread_b(down, c)
-        wait_b(up, 3 - c)
-        spread_b(up, 3 - c)
-    for c in (0, 3, 1, 2):
-        wait_b(far, c)
-        spread_b(far, c)
+    def gather(low):
+        count = {"a": 0, "b": 0}
+
+        def send(kind, part, ssem, rsem, device):
+            pltpu.make_async_remote_copy(
+                part, part, ssem.at[count[kind]], rsem, device_id=device, device_id_type=MESH
+            ).start()
+            count[kind] += 1
+
+        def b_to(r, h, c):
+            send("b", panel_b.at[h, c], send_b, recv_b.at[h, c], dev(r=r))
+
+        def along_x(half, g):
+            for d in (1, 3, 2):
+                send("a", panel_a.at[half, g], send_a, recv_a.at[half, g], dev(c=at_x(d)))
+
+        def along_y(half, g):
+            for d in (1, 3, 2):
+                send("a", panel_a.at[half, g], send_a, recv_a.at[half, g], dev(c=at_y(d)))
+
+        def pass_on_a(d):
+            wait_a(0, at_x(d))
+            along_y(0, at_x(d))
+            wait_a(1, at_y(d))
+            along_x(1, at_y(d))
+
+        def pass_on_b(source, c, r):
+            wait_b(source, c)
+            b_to(r, source, c)
+
+        def spread_own():
+            a_dup[16 * TA] = jnp.zeros((TILE, LANES), jnp.bfloat16)
+            for half in range(2):
+                spread_a(half, col)
+            for c in range(4):
+                spread_b(row, c)
+
+        if low:
+            pack_a(0)
+            pl.semaphore_wait(barrier, len(friends))
+            along_x(0, col)
+            pack_a(1)
+            along_y(1, col)
+            for c in (3, 2, 1, 0):
+                pack_b(c)
+                b_to(mate, row, c)
+            along_y(0, col)
+            along_x(1, col)
+            spread_own()
+            for d in (1, 3, 2):
+                pass_on_a(d)
+            pl.semaphore_wait(ready, 1)
+            for c in range(4):
+                b_to(cross, row, c)
+                if c not in LOW_BY_CROSS:
+                    pass_on_b(mate, c, cross)
+            for c in HIGH_BY_CROSS:
+                pass_on_b(cross, c, mate)
+        else:
+            pack_b(0)
+            pl.semaphore_wait(barrier, len(friends) + 1)
+            pl.semaphore_signal(ready, inc=1, device_id=dev(r=cross), device_id_type=MESH)
+            b_to(cross, row, 0)
+            pack_b(3)
+            b_to(mate, row, 3)
+            pack_b(1)
+            b_to(cross, row, 1)
+            pack_b(2)
+            b_to(cross, row, 2)
+            b_to(cross, row, 3)
+            pack_a(0)
+            along_x(0, col)
+            pack_a(1)
+            along_y(1, col)
+            along_y(0, col)
+            along_x(1, col)
+            for c in (0, 1, 2):
+                b_to(mate, row, c)
+            spread_own()
+            pass_on_a(1)
+            pass_on_a(3)
+            for c in range(4):
+                if c not in HIGH_BY_CROSS:
+                    pass_on_b(mate, c, cross)
+            pass_on_a(2)
+            for c in LOW_BY_CROSS:
+                pass_on_b(cross, c, mate)
+
+    @pl.when(is_low)
+    def _():
+        gather(True)
+
+    @pl.when(jnp.logical_not(is_low))
+    def _():
+        gather(False)
+
+    def later(low, source, c):
+        passed = HIGH_BY_CROSS if low else LOW_BY_CROSS
+        other = LOW_BY_CROSS if low else HIGH_BY_CROSS
+        return c not in passed if source == "cross" else c in other
+
+    def last_waits(low):
+        for d in (1, 3, 2):
+            spread_a(0, at_x(d))
+            spread_a(1, at_y(d))
+
+        def rest_of_a(d):
+            for e in (0, 1, 3, 2):
+                g = (cx + e) % 4 * 4 + (cy + d) % 4
+                wait_a(0, g)
+                spread_a(0, g)
+                g = (cx + d) % 4 * 4 + (cy + e) % 4
+                wait_a(1, g)
+                spread_a(1, g)
+
+        rest_of_a(1)
+        for c in range(4):
+            if later(low, "cross", c):
+                wait_b(cross, c)
+            spread_b(cross, c)
+            if later(low, "mate", c):
+                wait_b(mate, c)
+            spread_b(mate, c)
+        rest_of_a(3)
+        rest_of_a(2)
+        for c in range(4):
+            wait_b(far, c)
+            spread_b(far, c)
+
+    @pl.when(is_low)
+    def _():
+        last_waits(True)
+
+    @pl.when(jnp.logical_not(is_low))
+    def _():
+        last_waits(False)
+
     ai_in.wait()
     bi_in.wait()
 
@@ -292,8 +344,20 @@
     for j in range(PACK):
         out_ref[:, j * LANES:(j + 1) * LANES] = out_wide[pl.ds(j * OWNED, OWNED)].astype(jnp.bfloat16)
 
-    for cp in started:
-        cp.wait_send()
+    for i in range(N_SEND_A):
+        pltpu.make_async_copy(panel_a.at[0, 0], panel_a.at[0, 0], send_a.at[i]).wait()
+    def b_sent(first, last):
+        for i in range(first, last):
+            pltpu.make_async_copy(panel_b.at[0, 0], panel_b.at[0, 0], send_b.at[i]).wait()
+
+    @pl.when(is_low)
+    def _():
+        b_sent(0, N_LOW_B)
+
+    @pl.when(jnp.logical_not(is_low))
+    def _():
+        b_sent(0, N_HIGH_B)
+
     for i in range(n_peer):
         peer_copy(i).wait_send()
     for i in range(n_z):
@@ -328,9 +392,10 @@
             pltpu.VMEM((OWNED, PACK, LANES), bf16),
             pltpu.VMEM((PACK * OWNED, LANES), f32),
             pltpu.SemaphoreType.DMA((8,)),
-            pltpu.SemaphoreType.DMA((30,)),
+            pltpu.SemaphoreType.REGULAR,
+            pltpu.SemaphoreType.DMA((N_SEND_A,)),
             pltpu.SemaphoreType.DMA((2, 16)),
-            pltpu.SemaphoreType.DMA((12,)),
+            pltpu.SemaphoreType.DMA((16,)),
             pltpu.SemaphoreType.DMA((4, 4)),
             pltpu.SemaphoreType.DMA((len(PEER_CUTS),)),
             pltpu.SemaphoreType.DMA((len(PEER_CUTS),)),

time: 28.9 us -> 28.4 us (0.983)
  Pallas kernels: 28.1 us -> 27.6 us
    pallas_call x1, Pallas kernels: 28.1 us -> 27.6 us  [shards(): pl.pallas_call(kernel, out_shape=pltpu.VMEM((OWNED, flat), bf16), in_spec...]
where the time goes in v3:
time: 28.4 us; the launch traced here: 28.3 us
  Pallas kernels  27.6 us (97%)
  local copies, waits for them, and re-layouts  0.68 us (2%)
    pallas_call x1, Pallas kernels, shards(): pl.pallas_call(kernel, out_shape=pltpu.VMEM((OWNED, flat), bf16), in_spec...  27.6 us
    unnamed x1, local copies, waits for them, and re-layouts  0.68 us

profile of v3, /device:TPU:1, one launch (start us, length us, event | category | flops | bytes accessed | tf_op | source)
XLA Modules:
  0.0 28.3 jit_solution(14725134518143158595)
XLA Ops:
  0.0 27.6 %purify.1 = bf16[24,4096]{1,0:T(8,128)(2,1)S(1)} custom-call(bf16[8,4096]{1,0:T(8,128)(2,1)} %bitcast.7, bf16[16,4096]{1,0:T(8,128)(2,1)} %bitcast.6, s32[1,768]{1,0:T(1,128)} %bitcast.8, s32[1,768]{1,0:T(1,128)} %bitcast.9), custom_call_target="tpu_custom_call" | custom-call | tf_op jit(solution)/shard_map/purify/pallas_call | solution.py:370
  27.6 0.7 %copy.6 = bf16[1,1,24,4096]{3,2,1,0:T(8,128)(2,1)} copy(bf16[1,1,24,4096]{3,2,1,0:T(8,128)(2,1)S(1)} %bitcast.5) | data formatting | bytes 393216

commit v4 on v3

--- a/solution.py
+++ b/solution.py
@@ -21,7 +21,7 @@
 N_LOW_B = 12 + len(HIGH_BY_CROSS) - len(LOW_BY_CROSS)
 N_HIGH_B = 12 + len(LOW_BY_CROSS) - len(HIGH_BY_CROSS)
 Z_CUTS = ((0, 4), (4, 6), (10, 8), (18, 6))
-PEER_CUTS = Z_CUTS + ((24, 12), (36, 12))
+PEER_CUTS = Z_CUTS + ((24, 24),)
 
 
 def low_half(rows):
@@ -174,12 +174,14 @@
             for d in (1, 3, 2):
                 pass_on_a(d)
             pl.semaphore_wait(ready, 1)
-            for c in range(4):
-                b_to(cross, row, c)
-                if c not in LOW_BY_CROSS:
-                    pass_on_b(mate, c, cross)
-            for c in HIGH_BY_CROSS:
-                pass_on_b(cross, c, mate)
+            b_to(cross, row, 0)
+            b_to(cross, row, 1)
+            pass_on_b(cross, 0, mate)
+            b_to(cross, row, 2)
+            pass_on_b(cross, 1, mate)
+            pass_on_b(mate, 3, cross)
+            b_to(cross, row, 3)
+            pass_on_b(cross, 2, mate)
         else:
             pack_b(0)
             pl.semaphore_wait(barrier, len(friends) + 1)
@@ -315,18 +317,11 @@
         z_copy(i).start()
 
     n_z, n_peer = len(Z_CUTS), len(PEER_CUTS)
-    for_peer(0, g1)
-    for_z(0)
-    for_peer(1, g1)
-    for_z(1)
-    for_peer(2, g1)
-    for_z(2)
-    send_on(0)
-    send_on(1)
-    for_peer(3, g1)
-    for_z(3)
-    send_on(2)
-    send_on(3)
+    for i in range(n_z):
+        for_peer(i, g1)
+    for i in range(n_z):
+        for_z(i)
+        send_on(i)
     for i in range(n_z, n_peer):
         for_peer(i, g3)
     for s in range(OWNED):
@@ -336,6 +331,22 @@
         first, count = PEER_CUTS[i]
         for s in range(first, first + count):
             own_out[s - OWNED] += from_peer[s].astype(jnp.float32)
+    for i in range(N_SEND_A):
+        pltpu.make_async_copy(panel_a.at[0, 0], panel_a.at[0, 0], send_a.at[i]).wait()
+    def b_sent(first, last):
+        for i in range(first, last):
+            pltpu.make_async_copy(panel_b.at[0, 0], panel_b.at[0, 0], send_b.at[i]).wait()
+
+    @pl.when(is_low)
+    def _():
+        b_sent(0, N_LOW_B)
+
+    @pl.when(jnp.logical_not(is_low))
+    def _():
+        b_sent(0, N_HIGH_B)
+
+    for i in range(n_peer):
+        peer_copy(i).wait_send()
     for i in range(n_z):
         first, count = Z_CUTS[i]
         z_copy(i).wait_recv()
@@ -344,22 +355,6 @@
     for j in range(PACK):
         out_ref[:, j * LANES:(j + 1) * LANES] = out_wide[pl.ds(j * OWNED, OWNED)].astype(jnp.bfloat16)
 
-    for i in range(N_SEND_A):
-        pltpu.make_async_copy(panel_a.at[0, 0], panel_a.at[0, 0], send_a.at[i]).wait()
-    def b_sent(first, last):
-        for i in range(first, last):
-            pltpu.make_async_copy(panel_b.at[0, 0], panel_b.at[0, 0], send_b.at[i]).wait()
-
-    @pl.when(is_low)
-    def _():
-        b_sent(0, N_LOW_B)
-
-    @pl.when(jnp.logical_not(is_low))
-    def _():
-        b_sent(0, N_HIGH_B)
-
-    for i in range(n_peer):
-        peer_copy(i).wait_send()
     for i in range(n_z):
         z_copy(i).wait_send()
 

time: 28.4 us -> 28.3 us (level)
  no operation moved by 1% of the time
where the time goes in v4:
time: 28.3 us; the launch traced here: 28.2 us
  Pallas kernels  27.5 us (97%)
  local copies, waits for them, and re-layouts  0.68 us (2%)
    pallas_call x1, Pallas kernels, shards(): pl.pallas_call(kernel, out_shape=pltpu.VMEM((OWNED, flat), bf16), in_spec...  27.5 us
    unnamed x1, local copies, waits for them, and re-layouts  0.68 us

profile of v4, /device:TPU:1, one launch (start us, length us, event | category | flops | bytes accessed | tf_op | source)
XLA Modules:
  0.0 28.2 jit_solution(5753322476813320795)
XLA Ops:
  0.0 27.5 %purify.1 = bf16[24,4096]{1,0:T(8,128)(2,1)S(1)} custom-call(bf16[8,4096]{1,0:T(8,128)(2,1)} %bitcast.7, bf16[16,4096]{1,0:T(8,128)(2,1)} %bitcast.6, s32[1,768]{1,0:T(1,128)} %bitcast.8, s32[1,768]{1,0:T(1,128)} %bitcast.9), custom_call_target="tpu_custom_call" | custom-call | tf_op jit(solution)/shard_map/purify/pallas_call | solution.py:365
  27.5 0.7 %copy.6 = bf16[1,1,24,4096]{3,2,1,0:T(8,128)(2,1)} copy(bf16[1,1,24,4096]{3,2,1,0:T(8,128)(2,1)S(1)} %bitcast.5) | data formatting | bytes 393216

commit v5 on v4

--- a/solution.py
+++ b/solution.py
@@ -16,11 +16,10 @@
 B_COLS = 1024
 OWNED = 24
 N_SEND_A = 30
-HIGH_BY_CROSS = (0, 1, 2)
 LOW_BY_CROSS = (0, 1, 2)
-N_LOW_B = 12 + len(HIGH_BY_CROSS) - len(LOW_BY_CROSS)
-N_HIGH_B = 12 + len(LOW_BY_CROSS) - len(HIGH_BY_CROSS)
-Z_CUTS = ((0, 4), (4, 6), (10, 8), (18, 6))
+N_B = 11
+SPARE = 12
+Z_CUTS = ((0, 4), (4, 4), (8, 4), (12, 4), (16, 4), (20, 4))
 PEER_CUTS = Z_CUTS + ((24, 24),)
 
 
@@ -53,6 +52,7 @@
     partner = dev(l=(1 - zl) * 2 + core)
     mate, cross, far = row + 1 - 2 * (row % 2), 3 - row, (row + 2) % 4
     is_low = row < 2
+    mate_outer = zl == mate % 2
 
     barrier = pltpu.get_barrier_semaphore()
 
@@ -147,6 +147,12 @@
             along_y(0, at_x(d))
             wait_a(1, at_y(d))
             along_x(1, at_y(d))
+
+        def spare(source, c, r):
+            part = panel_b.at[source, c]
+            pltpu.make_async_remote_copy(
+                part, part, send_b.at[SPARE], recv_b.at[source, c], device_id=dev(r=r), device_id_type=MESH
+            ).start()
 
         def pass_on_b(source, c, r):
             wait_b(source, c)
@@ -174,14 +180,17 @@
             for d in (1, 3, 2):
                 pass_on_a(d)
             pl.semaphore_wait(ready, 1)
-            b_to(cross, row, 0)
-            b_to(cross, row, 1)
-            pass_on_b(cross, 0, mate)
-            b_to(cross, row, 2)
-            pass_on_b(cross, 1, mate)
-            pass_on_b(mate, 3, cross)
-            b_to(cross, row, 3)
-            pass_on_b(cross, 2, mate)
+            for c in range(4):
+                b_to(cross, row, c)
+                if c not in LOW_BY_CROSS:
+                    pass_on_b(mate, c, cross)
+            for c in (0, 1):
+                pass_on_b(cross, c, mate)
+            wait_b(cross, 2)
+
+            @pl.when(mate_outer)
+            def _():
+                spare(cross, 2, mate)
         else:
             pack_b(0)
             pl.semaphore_wait(barrier, len(friends) + 1)
@@ -193,6 +202,7 @@
             b_to(cross, row, 1)
             pack_b(2)
             b_to(cross, row, 2)
+            b_to(mate, row, 2)
             b_to(cross, row, 3)
             pack_a(0)
             along_x(0, col)
@@ -200,14 +210,18 @@
             along_y(1, col)
             along_y(0, col)
             along_x(1, col)
-            for c in (0, 1, 2):
+            for c in (0, 1):
                 b_to(mate, row, c)
             spread_own()
             pass_on_a(1)
             pass_on_a(3)
-            for c in range(4):
-                if c not in HIGH_BY_CROSS:
-                    pass_on_b(mate, c, cross)
+            pass_on_b(mate, 3, cross)
+            wait_b(mate, 2)
+
+            @pl.when(jnp.logical_not(mate_outer))
+            def _():
+                spare(mate, 2, cross)
+
             pass_on_a(2)
             for c in LOW_BY_CROSS:
                 pass_on_b(cross, c, mate)
@@ -221,9 +235,9 @@
         gather(False)
 
     def later(low, source, c):
-        passed = HIGH_BY_CROSS if low else LOW_BY_CROSS
-        other = LOW_BY_CROSS if low else HIGH_BY_CROSS
-        return c not in passed if source == "cross" else c in other
+        if source == "cross":
+            return c == 3
+        return c < 3 if low else c < 2
 
     def last_waits(low):
         for d in (1, 3, 2):
@@ -337,13 +351,15 @@
         for i in range(first, last):
             pltpu.make_async_copy(panel_b.at[0, 0], panel_b.at[0, 0], send_b.at[i]).wait()
 
-    @pl.when(is_low)
-    def _():
-        b_sent(0, N_LOW_B)
+    b_sent(0, N_B)
 
     @pl.when(jnp.logical_not(is_low))
     def _():
-        b_sent(0, N_HIGH_B)
+        b_sent(N_B, SPARE)
+
+    @pl.when(is_low == mate_outer)
+    def _():
+        b_sent(SPARE, SPARE + 1)
 
     for i in range(n_peer):
         peer_copy(i).wait_send()
@@ -390,7 +406,7 @@
             pltpu.SemaphoreType.REGULAR,
             pltpu.SemaphoreType.DMA((N_SEND_A,)),
             pltpu.SemaphoreType.DMA((2, 16)),
-            pltpu.SemaphoreType.DMA((16,)),
+            pltpu.SemaphoreType.DMA((SPARE + 1,)),
             pltpu.SemaphoreType.DMA((4, 4)),
             pltpu.SemaphoreType.DMA((len(PEER_CUTS),)),
             pltpu.SemaphoreType.DMA((len(PEER_CUTS),)),

time: 28.3 us -> 28.2 us (level)
  no operation moved by 1% of the time
where the time goes in v5:
time: 28.2 us; the launch traced here: 28.1 us
  Pallas kernels  27.4 us (97%)
  local copies, waits for them, and re-layouts  0.68 us (2%)
    pallas_call x1, Pallas kernels, shards(): pl.pallas_call(kernel, out_shape=pltpu.VMEM((OWNED, flat), bf16), in_spec...  27.4 us
    unnamed x1, local copies, waits for them, and re-layouts  0.68 us

profile of v5, /device:TPU:1, one launch (start us, length us, event | category | flops | bytes accessed | tf_op | source)
XLA Modules:
  0.0 28.1 jit_solution(4856146300369697057)
XLA Ops:
  0.0 27.4 %purify.1 = bf16[24,4096]{1,0:T(8,128)(2,1)S(1)} custom-call(bf16[8,4096]{1,0:T(8,128)(2,1)} %bitcast.7, bf16[16,4096]{1,0:T(8,128)(2,1)} %bitcast.6, s32[1,768]{1,0:T(1,128)} %bitcast.8, s32[1,768]{1,0:T(1,128)} %bitcast.9), custom_call_target="tpu_custom_call" | custom-call | tf_op jit(solution)/shard_map/purify/pallas_call | solution.py:381
  27.4 0.7 %copy.6 = bf16[1,1,24,4096]{3,2,1,0:T(8,128)(2,1)} copy(bf16[1,1,24,4096]{3,2,1,0:T(8,128)(2,1)S(1)} %bitcast.5) | data formatting | bytes 393216
